TPU v7x, 512 devices: a whole 4x8x8 slice. The times are simulated.
512 devices in a mesh: rows: 64 (over z, y), feat: 8 (over x, core).
Axes of the slice: x: 4, y: 8, z: 8, core: 2. Of those that a mesh axis runs over, the one named last changes fastest.
Arguments:
- predictions: bfloat16 [98304, 4096], P('rows', 'feat'), may hold values from -9 to 9
- targets: bfloat16 [98304, 4096], P('rows', 'feat'), may hold values from 0 to 1
- sketch_matrix: bfloat16 [32, 4096], P(None, 'feat'), may hold values from -0.0048828125 to 0.0048828125
- bin_codes: int32 [256, 98304], P('feat', 'rows'), may hold values from 0 to 255
- row_node: int32 [98304], P('rows'), may hold values from 0 to 3
- smaller: int32 [4], replicated, may hold values from 0 to 1, as said below
- split_feature: int32 [4], replicated, may hold values from 0 to 255
- split_bin: int32 [4], replicated, may hold values from 64 to 191
Outputs:
- new_predictions: bfloat16 [98304, 4096], P('rows', 'feat')
- histograms: float32 [256, 16384], P('rows', 'feat')
Inputs may be any that keep to these rules, and one draw needn't show every extreme that they name: Of the nodes 2 p and 2 p + 1 exactly one has smaller equal to 1.
All inputs are finite; a program needn't handle non-finite values.
Results may differ from a plain program's by a relative error of at most 0.0034.
Values sent between devices are 32-bit elements; how exact they have to be, the bound alone decides.
A program may use at most 64 MiB of HBM per device.

v0:
```python
import math

import jax
import jax.numpy as jnp
from jax import lax
from jax.sharding import PartitionSpec as P

BINS = 256


DAMPING = 1.0
SHRINKAGE = 0.5


def per_device(
    predictions, targets, sketch_matrix, bin_codes, row_node, smaller, split_feature, split_bin
):
    row_count = predictions.shape[0]
    feat_dev = bin_codes.shape[0]
    node_total = smaller.shape[0]
    slot_total = node_total // 2
    leaf_total = 2 * node_total
    column_dev = lax.axis_index("feat")
    logits = predictions.astype(jnp.float32)
    probability = jax.nn.sigmoid(logits)
    gradient = (probability - targets.astype(jnp.float32)).astype(jnp.bfloat16)
    hessian = (probability * (1.0 - probability)).astype(jnp.bfloat16)
    partial_value = lax.dot_general(
        gradient, sketch_matrix, (((1,), (1,)), ((), ())), preferred_element_type=jnp.float32
    )
    node_hot = (row_node[:, None] == jnp.arange(node_total, dtype=jnp.int32)[None, :]).astype(
        jnp.int32
    )
    feat_row = jnp.sum(node_hot * split_feature[None, :], axis=1)
    thresh_row = jnp.sum(node_hot * split_bin[None, :], axis=1)
    small_row = jnp.sum(node_hot * smaller[None, :], axis=1)
    local_feat = feat_row - column_dev * feat_dev
    selector = jnp.arange(feat_dev, dtype=jnp.int32)[:, None] == local_feat[None, :]
    code_at = jnp.sum(jnp.where(selector, bin_codes, 0), axis=0)
    owned = jnp.any(selector, axis=0)
    right_part = jnp.where(owned & (code_at > thresh_row), 1.0, 0.0).astype(jnp.float32)
    sketch, right_side = lax.psum((partial_value, right_part), "feat")
    leaf_id = 2 * row_node + (right_side > 0.5).astype(jnp.int32)
    slot_mask = ((row_node // 2)[:, None] == jnp.arange(slot_total, dtype=jnp.int32)[None, :]) & (
        small_row == 1
    )[:, None]
    weighted = (
        (slot_mask.astype(jnp.float32)[:, :, None] * sketch[:, None, :])
        .reshape(row_count, -1)
        .astype(jnp.bfloat16)
    )
    width = weighted.shape[1]
    group_size = math.gcd(feat_dev, 8)
    grouped = bin_codes.reshape(feat_dev // group_size, group_size, row_count)
    bin_ids = jnp.arange(BINS, dtype=jnp.int32)

    def one_group(codes_group):
        one_hot = (codes_group[:, None, :] == bin_ids[None, :, None]).astype(jnp.bfloat16)
        return lax.dot_general(
            one_hot, weighted, (((2,), (0,)), ((), ())), preferred_element_type=jnp.float32
        )

    stacked = lax.map(one_group, grouped).reshape(feat_dev, BINS, width)
    histograms = lax.psum_scatter(
        stacked.transpose(1, 0, 2).reshape(BINS, feat_dev * width),
        "rows",
        scatter_dimension=0,
        tiled=True,
    )
    leaf_match = jnp.arange(leaf_total, dtype=jnp.int32)[:, None] == leaf_id[None, :]
    leaf_hot = leaf_match.astype(jnp.bfloat16)
    grad_sum = jnp.dot(leaf_hot, gradient, preferred_element_type=jnp.float32)
    hess_sum = jnp.dot(leaf_hot, hessian, preferred_element_type=jnp.float32)
    grad_own, hess_own = (
        lax.psum_scatter(grad_sum, "rows", scatter_dimension=1, tiled=True),
        lax.psum_scatter(hess_sum, "rows", scatter_dimension=1, tiled=True),
    )
    owned_values = -grad_own / (hess_own + DAMPING)
    values = lax.all_gather(owned_values, "rows", axis=1, tiled=True)
    update = jnp.dot(leaf_match.T.astype(jnp.float32), values, precision=lax.Precision.HIGHEST)
    new_predictions = (logits + SHRINKAGE * update).astype(jnp.bfloat16)
    return (new_predictions, histograms)


def solution(mesh):
    placed = (
        P("rows", "feat"),
        P("rows", "feat"),
        P(None, "feat"),
        P("feat", "rows"),
        P("rows"),
        P(),
        P(),
        P(),
    )
    return jax.shard_map(
        per_device,
        mesh=mesh,
        in_specs=placed,
        out_specs=(P("rows", "feat"), P("rows", "feat")),
        check_vma=False,
    )
```

profile of v0, /device:TPU:8, one launch (start us, length us, event | category | flops | bytes accessed | tf_op | source)
XLA Modules:
  0.0 445.8 jit_solution(7354228785645584075)
XLA Ops:
  7.2 0.0 copy-start
  7.2 0.0 copy-start.3
  7.2 0.0 all-reduce.7.cloned.1.call-start
  7.3 2.9 subtract_convert_fusion
  10.2 0.0 copy-done
  10.2 0.0 copy-start.2
  10.2 1.2 fusion.28
  11.4 0.0 all-reduce.7.cloned.1.call-update
  11.5 0.0 all-reduce.9.cloned.1.call-start
  11.5 0.1 select_reduce_fusion.1
  11.8 14.9 %psum.14 = f32[1536]{0:T(1024)S(1)} all-reduce(f32[1536]{0:T(1024)S(1)} %and_select_fusion), channel_id=1, replica_groups=mesh['rows'=64,'feat'=8] {'feat'}, use_global_device_ids=true, to_apply=%region_4.5 | all-reduce | flops 1536 | bytes 12288 | tf_op jit(solution)/shard_map/psum | solution.py:42
  26.7 59.8 %all-reduce.7.cloned.1.call-done = f32[1536,32]{0,1:T(8,128)} async-done(((f32[1536,32]{0,1:T(8,128)}), f32[1536,32]{0,1:T(8,128)}) %all-reduce.7.cloned.1.call-update) | async-done | bytes 196624 | tf_op jit(solution)/shard_map/psum | solution.py:42
  86.5 16.0 %while.11 = (s32[]{:T(128)}, f32[4,8,256,64]{2,3,1,0:T(8,128)}, s32[4,8,1536]{2,1,0:T(8,128)S(1)}, f32[1536,32]{0,1:T(8,128)}, f32[1536,2]{0,1:T(2,128)S(1)}, /*index=5*/s32[]{:T(128)}) while((s32[]{:T(128)}, f32[4,8,256,64]{2,3,1,0:T(8,128)}, s32[4,8,1536]{2,1,0:T(8,128)S(1)}, f32[1536,32]{0,1:T(8,128)}, ...), condition=%wide.region_10.11_spmd.clone, body=%wide.region_9.10_spmd.clone.sunk | while | flops 405995520 | bytes 1274441 | solution.py:63
  86.5 1.0 multiply_convert_fusion.2
  87.5 3.0 fusion.37
  90.5 1.0 multiply_convert_fusion.2
  91.5 3.1 fusion.37
  94.5 1.0 multiply_convert_fusion.2
  95.5 3.0 fusion.37
  98.5 1.0 multiply_convert_fusion.2
  99.5 3.1 fusion.37
  102.5 0.0 all-reduce.9.cloned.1.call-update
  102.6 1.4 dynamic-slice
  104.6 0.3 fusion.19
  104.9 0.9 fusion.13
  105.9 275.4 %all-reduce.3 = (f32[8,512]{1,0:T(8,128)S(1)}, f32[8,512]{1,0:T(8,128)S(1)}) all-reduce(f32[8,512]{1,0:T(8,128)S(1)} %fusion.13, f32[8,512]{1,0:T(8,128)S(1)} %fusion.19), channel_id=3, replica_groups=mesh['rows'=64,'feat'=8] {'rows'}, use_global_device_ids=true, to_apply=%region_6.7.clone | all-reduce | flops 8192 | bytes 65536
  381.3 0.1 fusion.26
  381.4 0.1 copy.14
  382.1 51.7 %all_gather.3 = f32[8,512]{0,1:T(8,128)S(1)} all-gather(f32[8,8]{0,1:T(8,128)S(1)} %copy.14), channel_id=1, replica_groups=mesh['rows'=64,'feat'=8] {'rows'}, dimensions={1}, use_global_device_ids=true | all-gather | bytes 16640 | tf_op jit(solution)/shard_map/all_gather | solution.py:79
  433.8 2.7 fusion.12
  436.5 1.6 constant_dynamic-slice_fusion
  438.1 0.9 copy.15
  (23 shorter events, 0.2 us)
Async XLA Ops:
  7.2 3.0 copy-start
  7.2 4.3 copy-start.3
  7.2 4.3 copy-start.4
  7.2 4.3 copy-start.5
  7.2 4.3 copy-start.6
  7.2 79.3 %all-reduce.7.cloned.1.call-start = ((), (), s32[]{:S(2)}) async-start(), calls=%async_computation | async-start | bytes 393216 | tf_op jit(solution)/shard_map/psum | solution.py:42
  10.2 1.6 copy-start.2
  11.5 425.1 %all-reduce.9.cloned.1.call-start = ((), (), s32[]{:S(2)}) async-start(), calls=%async_computation.1 | async-start | bytes 4194304
  102.5 2.4 copy-start.1
Sparse Core Ops, SparseCore 0:
  11.6 74.8 all-reduce.6
  102.7 162.4 all-reduce.8
where the time goes:
time: 446 us
  blocking collectives  342 us (77%)
  waiting for transfers between devices  59.8 us (13%)
  matrix products  17.4 us (4%)
  between operations  15.5 us (3%)
  other arithmetic  7.02 us (2%)
    unnamed x1, blocking collectives  275 us
    psum x1, waiting for transfers between devices, per_device(): sketch, right_side = lax.psum((partial_value, right_part), 'feat')  59.8 us
    all_gather x1, blocking collectives, per_device(): values = lax.all_gather(owned_values, 'rows', axis=1, tiled=True)  51.7 us
    psum x1, blocking collectives, per_device(): sketch, right_side = lax.psum((partial_value, right_part), 'feat')  14.9 us
    dot_general x4, matrix products, one_group(): lax.dot_general(one_hot, weighted, (((2,), (0,)), ((), ())), preferred_el...  12.2 us
  transfers between devices with their start and end apart: 2, of which 1 were waited for; matrix products, arithmetic and copies ran while one was open for 1% of the time, Pallas kernels for 0%

commit v1 on v0

v1 whole, which is shorter than its diff:
```python
import functools
import math

import jax
import jax.numpy as jnp
from jax import lax
from jax.experimental import pallas as pl
from jax.experimental.pallas import tpu as pltpu
from jax.sharding import PartitionSpec as P

BINS = 256
DAMPING = 1.0
SHRINKAGE = 0.5
SIDES = 2
GROUP = 2
CHUNK = 256
BLOCK = 64
MESH = pl.DeviceIdType.MESH


def kernel(
    side,
    feat_total,
    pred_hbm,
    targ_hbm,
    sketch_ref,
    codes_ref,
    node_ref,
    smaller_ref,
    feature_ref,
    bin_ref,
    newp_hbm,
    hist_ref,
    pred,
    targ,
    grad,
    hess,
    part,
    part_in,
    sketch,
    right,
    right_in,
    weights,
    codes,
    bins,
    hist,
    ring_in,
    last_out,
    last_in,
    leaf_out,
    leaf_in,
    leaf_sum,
    leaf_sum_in,
    value_own,
    value_in,
    values,
    leaf_hot,
    newp,
    load_sem,
    store_sem,
    right_send,
    right_recv,
    part_send,
    part_recv,
    sketch_send,
    sketch_recv,
    ring_send,
    ring_recv,
    last_send,
    last_recv,
    leaf_send,
    leaf_recv,
):
    row_count, label_count = grad.shape
    chunks = row_count // CHUNK
    feats = codes_ref.shape[0]
    nodes = smaller_ref.shape[0]
    leaves = 2 * nodes
    columns = sketch_ref.shape[0]
    groups = hist.shape[0] // GROUP
    half = side // 2
    owned_bins = BINS // (side * side)
    ring_bins = BINS // side
    leaf_part = leaves // side

    here = lax.axis_index("rows")
    me_z = here // side
    me_y = here % side
    me_f = lax.axis_index("feat")

    def at_y(k):
        return {"rows": me_z * side + (me_y + k + side) % side}

    def at_z(k):
        return {"rows": ((me_z + k + side) % side) * side + me_y}

    def at_f(k):
        return {"feat": (me_f + k) % feat_total}

    def remote(src, dst, send, recv, where):
        return pltpu.make_async_remote_copy(
            src_ref=src,
            dst_ref=dst,
            send_sem=send,
            recv_sem=recv,
            device_id=where,
            device_id_type=MESH,
        )

    def loads(c):
        rows = pl.ds(c * CHUNK, CHUNK)
        return (
            pltpu.make_async_copy(pred_hbm.at[rows], pred.at[rows], load_sem.at[0, c]),
            pltpu.make_async_copy(targ_hbm.at[rows], targ.at[rows], load_sem.at[1, c]),
        )

    for c in range(chunks):
        for copy in loads(c):
            copy.start()

    barrier = pltpu.get_barrier_semaphore()
    for k in range(1, feat_total):
        pl.semaphore_signal(barrier, inc=1, device_id=at_f(k), device_id_type=MESH)
    for k in range(1, side):
        pl.semaphore_signal(barrier, inc=1, device_id=at_y(k), device_id_type=MESH)
        pl.semaphore_signal(barrier, inc=1, device_id=at_z(k), device_id_type=MESH)

    node = node_ref[...]
    right_part = jnp.zeros((1, row_count), jnp.float32)
    for n in range(nodes):
        local = feature_ref[n] - me_f * feats
        mine = (local >= 0) & (local < feats)
        row = codes_ref[pl.ds(jnp.clip(local, 0, feats - 1), 1), :]
        limit = jnp.where(mine, bin_ref[n], BINS)
        right_part += jnp.where((node == n) & (row > limit), 1.0, 0.0)
    right[...] = right_part

    codes[...] = codes_ref[...].astype(jnp.float32)
    place = lax.broadcasted_iota(jnp.int32, (BINS, 128), 0)
    major, rest = place // ring_bins, place % ring_bins
    minor, low = rest // owned_bins, rest % owned_bins
    bins[0] = ((minor * side + major) * owned_bins + low).astype(jnp.float32).astype(jnp.bfloat16)
    bins[1] = place.astype(jnp.float32).astype(jnp.bfloat16)

    def elementwise(c):
        for copy in loads(c):
            copy.wait()

        def block(b, carry):
            rows = pl.ds(pl.multiple_of(c * CHUNK + b * BLOCK, BLOCK), BLOCK)
            logits = pred[rows, :].astype(jnp.float32)
            prob = 0.5 * jnp.tanh(0.5 * logits) + 0.5
            grad[rows, :] = (prob - targ[rows, :].astype(jnp.float32)).astype(jnp.bfloat16)
            hess[rows, :] = (prob * (1.0 - prob)).astype(jnp.bfloat16)
            return carry

        lax.fori_loop(0, CHUNK // BLOCK, block, 0)
        rows = pl.ds(c * CHUNK, CHUNK)
        part[:, rows] = lax.dot_general(
            sketch_ref[...],
            grad[rows, :],
            (((1,), (1,)), ((), ())),
            preferred_element_type=jnp.float32,
        )

    def right_copy(k):
        return remote(right, right_in.at[k], right_send.at[k], right_recv.at[k], at_f(k))

    for c in range(chunks // 2):
        elementwise(c)
    pl.semaphore_wait(barrier, feat_total - 1 + 2 * (side - 1))
    for k in range(1, feat_total):
        right_copy(k).start()
    for c in range(chunks // 2, chunks):
        elementwise(c)

    piece_rows, piece_lanes = part_in.shape[1:]
    lane_parts = row_count // piece_lanes

    def piece(f):
        return (
            pl.ds(pl.multiple_of((f // lane_parts) * piece_rows, piece_rows), piece_rows),
            pl.ds(pl.multiple_of((f % lane_parts) * piece_lanes, 128), piece_lanes),
        )

    def part_copy(k):
        return remote(
            part.at[piece((me_f + k) % feat_total)],
            part_in.at[k],
            part_send.at[k],
            part_recv.at[k],
            at_f(k),
        )

    def sketch_copy(k, owner):
        return remote(
            sketch.at[piece(owner)],
            sketch.at[piece(owner)],
            sketch_send.at[k],
            sketch_recv.at[k],
            at_f(k),
        )

    for k in range(1, feat_total):
        part_copy(k).start()

    side_of = right_part
    for k in range(1, feat_total):
        right_copy(k).wait()
        side_of = side_of + right_in[k]
    leaf_id = 2 * node + (side_of > 0.5).astype(jnp.int32)
    tall = lax.broadcasted_iota(jnp.int32, (128, row_count), 0)
    hot = jnp.where((tall % leaves == leaf_id) & (tall < 3 * leaves), 1.0, 0.0)
    leaf_hot[...] = hot.T.astype(jnp.bfloat16)
    wide = hot[:leaves].astype(jnp.bfloat16)
    grad_sum = jnp.dot(wide, grad[...], preferred_element_type=jnp.float32)
    hess_sum = jnp.dot(wide, hess[...], preferred_element_type=jnp.float32)
    for i in range(side):
        leaf_out[i, :leaf_part, :] = grad_sum[i * leaf_part : (i + 1) * leaf_part]
        leaf_out[i, leaf_part:, :] = hess_sum[i * leaf_part : (i + 1) * leaf_part]

    def leaf_copy(k):
        return remote(
            leaf_out.at[(me_y + k) % side],
            leaf_in.at[k],
            leaf_send.at[0, k],
            leaf_recv.at[0, k],
            at_y(k),
        )

    def leaf_sum_copy(k):
        return remote(
            leaf_sum, leaf_sum_in.at[k], leaf_send.at[1, k], leaf_recv.at[1, k], at_z(k)
        )

    def value_copy(k):
        return remote(value_own, value_in.at[k], leaf_send.at[2, k], leaf_recv.at[2, k], at_y(k))

    for k in range(1, side):
        leaf_copy(k).start()

    mine = part[piece(me_f)]
    for k in range(1, feat_total):
        part_copy(k).wait()
        mine = mine + part_in[k]
    sketch[piece(me_f)] = mine
    for k in range(1, feat_total):
        sketch_copy(k, me_f).start()

    total = leaf_out[me_y]
    for k in range(1, side):
        leaf_copy(k).wait()
        total = total + leaf_in[k]
    leaf_sum[...] = total
    for k in range(1, side):
        leaf_sum_copy(k).start()

    for k in range(1, feat_total):
        sketch_copy(k, me_f).wait_send()
        sketch_copy(k, (me_f - k + feat_total) % feat_total).wait_recv()

    full = sketch[...]
    zeros = jnp.zeros_like(full)
    slots = []
    for s in range(nodes // 2):
        keep = jnp.zeros((1, row_count), jnp.float32)
        for n in (2 * s, 2 * s + 1):
            keep += jnp.where((node == n) & (smaller_ref[n] == 1), 1.0, 0.0)
        slots.append(full * keep)
    first = jnp.concatenate(slots + [zeros] * len(slots), axis=0)
    weights[0] = first.T.astype(jnp.bfloat16)
    second = jnp.concatenate([zeros] * len(slots) + slots, axis=0)
    weights[1] = second.T.astype(jnp.bfloat16)

    lane_tiles = row_count // 128

    def one_hot(feature, turn):
        row = codes[pl.ds(feature, 1), :]
        tile = jnp.broadcast_to(row, (16, row_count)).astype(jnp.bfloat16)
        wanted = jnp.concatenate([tile] * (BINS // 16), axis=0)
        ids = jnp.concatenate([bins[turn]] * lane_tiles, axis=1)
        return jnp.where(ids == wanted, jnp.bfloat16(1), jnp.bfloat16(0))

    def compute(u):
        turn = u % SIDES

        def pair(i, carry):
            j = u * GROUP + i
            hist[j] = jnp.dot(
                one_hot(2 * j, turn), weights[0], preferred_element_type=jnp.float32
            ) + jnp.dot(
                one_hot(2 * j + 1, turn), weights[1], preferred_element_type=jnp.float32
            )
            return carry

        lax.fori_loop(0, GROUP, pair, 0)

    def ring_place(u):
        return (1 - u % SIDES) * me_y + (u % SIDES) * me_z

    def ring_peer(u, k):
        along_y = me_z * side + (me_y + k + side) % side
        along_z = ((me_z + k + side) % side) * side + me_y
        return {"rows": (1 - u % SIDES) * along_y + (u % SIDES) * along_z}

    def ring_rows(target):
        return pl.ds(pl.multiple_of((target + side) % side * ring_bins, ring_bins), ring_bins)

    def ring_copies(u, step):
        me = ring_place(u)
        copies = []
        for way, sign in ((0, 1), (1, -1)):
            first, count = (way, 1) if step == 0 else (0, GROUP)
            pairs = GROUP // 2 if step == 0 else GROUP
            start = way * pairs if step == 0 else 0
            copies.append(
                remote(
                    hist.at[
                        pl.ds(u * GROUP + start, pairs),
                        ring_rows(me + sign * (half - step)),
                    ],
                    ring_in.at[u, way, step, pl.ds(start, pairs)],
                    ring_send.at[u, way, step],
                    ring_recv.at[u, way, step],
                    ring_peer(u, sign),
                )
            )
        return copies

    def arrived(u, way, step):
        pairs = GROUP // 2 if step == 0 else GROUP
        start = way * pairs if step == 0 else 0
        return start, pairs, ring_in[u, way, step, start : start + pairs]

    def last_copy(u, k):
        to = (1 - u % SIDES) * me_z + (u % SIDES) * me_y
        return remote(
            last_out.at[u, (to + k) % side],
            last_in.at[u, k],
            last_send.at[u, k],
            last_recv.at[u, k],
            ring_peer(u + 1, k),
        )

    def stage(u, k):
        me = ring_place(u)
        if 1 <= k <= half:
            for copy in ring_copies(u, k - 1):
                copy.wait()
        if 1 <= k < half:
            for way, sign in ((0, 1), (1, -1)):
                start, pairs, value = arrived(u, way, k - 1)
                spot = (
                    pl.ds(u * GROUP + start, pairs),
                    ring_rows(me + sign * (half - k)),
                    slice(None),
                )
                hist[spot] = hist[spot] + value
        if k < half:
            for copy in ring_copies(u, k):
                copy.start()
        if k == half:
            for way in (0, 1):
                start, pairs, value = arrived(u, way, half - 1)
                spot = (pl.ds(u * GROUP + start, pairs), ring_rows(me), slice(None))
                hist[spot] = hist[spot] + value
            total = hist[pl.ds(u * GROUP, GROUP), ring_rows(me), :]
            for i in range(side):
                last_out[u, i] = total[:, i * owned_bins : (i + 1) * owned_bins]
            for i in range(1, side):
                last_copy(u, i).start()
        if k == half + 1:
            to = (1 - u % SIDES) * me_z + (u % SIDES) * me_y
            total = last_out[u, to]
            for i in range(1, side):
                last_copy(u, i).wait()
                total = total + last_in[u, i]
            for i in range(GROUP):
                lanes = pl.ds(pl.multiple_of((u * GROUP + i) * 128, 128), 128)
                hist_ref[:, lanes] = total[i]

    def update(c):
        rows = pl.ds(pl.multiple_of(c * CHUNK, CHUNK), CHUNK)
        moved = jnp.dot(leaf_hot[rows, :], values[...], preferred_element_type=jnp.float32)
        newp[rows, :] = (pred[rows, :].astype(jnp.float32) + SHRINKAGE * moved).astype(
            jnp.bfloat16
        )
        pltpu.make_async_copy(newp.at[rows], newp_hbm.at[rows], store_sem.at[c]).start()

    stages = half + 2
    slots_total = groups + stages - 1
    update_from = slots_total - chunks

    def slot(t, carry):
        @pl.when(t < groups)
        def _():
            compute(t)

        for k in range(stages):

            @pl.when((t >= k) & (t < groups + k))
            def _(k=k):
                stage(t - k, k)

        @pl.when(t == 0)
        def _():
            total = leaf_sum[...]
            for k in range(1, side):
                leaf_sum_copy(k).wait()
                total = total + leaf_sum_in[k]
            value_own[...] = -total[:leaf_part] / (total[leaf_part:] + DAMPING)
            for k in range(1, side):
                value_copy(k).start()

        @pl.when(t == 2)
        def _():
            for k in range(1, side):
                value_copy(k).wait()
            who = lax.broadcasted_iota(jnp.int32, (leaves, label_count), 0) // leaf_part
            found = jnp.zeros((leaves, label_count), jnp.float32)
            for k in range(side):
                owner = (me_y - k + side) % side
                row = value_own[...] if k == 0 else value_in[k]
                tiled = jnp.concatenate([row] * side, axis=0)
                found = jnp.where(who == owner, tiled, found)
            high = found.astype(jnp.bfloat16)
            rest = found - high.astype(jnp.float32)
            middle = rest.astype(jnp.bfloat16)
            rest = rest - middle.astype(jnp.float32)
            three = jnp.concatenate([high.astype(jnp.float32), middle.astype(jnp.float32), rest], 0)
            pad = jnp.zeros((128 - 3 * leaves, label_count), jnp.float32)
            values[...] = jnp.concatenate([three, pad], 0).astype(jnp.bfloat16)

        @pl.when(t >= update_from)
        def _():
            update(t - update_from)

        return carry

    lax.fori_loop(0, slots_total, slot, 0)
    for c in range(chunks):
        rows = pl.ds(c * CHUNK, CHUNK)
        pltpu.make_async_copy(newp.at[rows], newp_hbm.at[rows], store_sem.at[c]).wait()


def per_device(
    side,
    feat_total,
    predictions,
    targets,
    sketch_matrix,
    bin_codes,
    row_node,
    smaller,
    split_feature,
    split_bin,
):
    row_count, label_count = predictions.shape
    columns = sketch_matrix.shape[0]
    feats = bin_codes.shape[0]
    pairs = feats // 2
    groups = pairs // GROUP
    half = side // 2
    owned_bins = BINS // (side * side)
    leaves = 2 * smaller.shape[0]
    leaf_part = leaves // side
    chunks = row_count // CHUNK
    lane_parts = max(1, feat_total * 8 // columns)
    piece = (columns * lane_parts // feat_total, row_count // lane_parts)
    vmem = pltpu.VMEM
    bf16, f32 = jnp.bfloat16, jnp.float32
    dma = pltpu.SemaphoreType.DMA
    whole = pl.BlockSpec(memory_space=pltpu.VMEM)
    scalar = pl.BlockSpec(memory_space=pltpu.SMEM)
    anywhere = pl.BlockSpec(memory_space=pl.ANY)
    return pl.pallas_call(
        functools.partial(kernel, side, feat_total),
        out_shape=(
            jax.ShapeDtypeStruct((row_count, label_count), bf16),
            jax.ShapeDtypeStruct((owned_bins, pairs * 128), f32),
        ),
        in_specs=[anywhere, anywhere, whole, whole, whole, scalar, scalar, scalar],
        out_specs=(anywhere, whole),
        scratch_shapes=[
            vmem((row_count, label_count), bf16),
            vmem((row_count, label_count), bf16),
            vmem((row_count, label_count), bf16),
            vmem((row_count, label_count), bf16),
            vmem((columns, row_count), f32),
            vmem((feat_total,) + piece, f32),
            vmem((columns, row_count), f32),
            vmem((1, row_count), f32),
            vmem((feat_total, 1, row_count), f32),
            vmem((2, row_count, 128), bf16),
            vmem((feats, row_count), f32),
            vmem((2, BINS, 128), bf16),
            vmem((pairs, BINS, 128), f32),
            vmem((groups, 2, half, GROUP, BINS // side, 128), f32),
            vmem((groups, side, GROUP, owned_bins, 128), f32),
            vmem((groups, side, GROUP, owned_bins, 128), f32),
            vmem((side, 2 * leaf_part, label_count), f32),
            vmem((side, 2 * leaf_part, label_count), f32),
            vmem((2 * leaf_part, label_count), f32),
            vmem((side, 2 * leaf_part, label_count), f32),
            vmem((leaf_part, label_count), f32),
            vmem((side, leaf_part, label_count), f32),
            vmem((128, label_count), bf16),
            vmem((row_count, 128), bf16),
            vmem((row_count, label_count), bf16),
            dma((2, chunks)),
            dma((chunks,)),
            dma((feat_total,)),
            dma((feat_total,)),
            dma((feat_total,)),
            dma((feat_total,)),
            dma((feat_total,)),
            dma((feat_total,)),
            dma((groups, 2, half)),
            dma((groups, 2, half)),
            dma((groups, side)),
            dma((groups, side)),
            dma((3, side)),
            dma((3, side)),
        ],
        compiler_params=pltpu.CompilerParams(
            collective_id=0, has_side_effects=True, vmem_limit_bytes=48 << 20
        ),
        name="boost",
    )(
        predictions,
        targets,
        sketch_matrix,
        bin_codes,
        row_node.reshape(1, row_count),
        smaller,
        split_feature,
        split_bin,
    )


def solution(mesh):
    placed = (
        P("rows", "feat"),
        P("rows", "feat"),
        P(None, "feat"),
        P("feat", "rows"),
        P("rows"),
        P(),
        P(),
        P(),
    )
    side = math.isqrt(mesh.shape["rows"])
    return jax.shard_map(
        functools.partial(per_device, side, mesh.shape["feat"]),
        mesh=mesh,
        in_specs=placed,
        out_specs=(P("rows", "feat"), P("rows", "feat")),
        check_vma=False,
    )
```

time: 446 us -> 81.6 us (0.18)
  blocking collectives: 342 us -> 0 us
  Pallas kernels: 0 us -> 71.7 us
  waiting for transfers between devices: 59.8 us -> 0 us
  matrix products: 17.4 us -> 0 us
  between operations: 15.5 us -> 0.65 us
  other arithmetic: 7.02 us -> 0 us
  local copies, waits for them, and re-layouts: 4.01 us -> 8.92 us
    unnamed x1 -> x0, blocking collectives: 275 us -> none
    pallas_call x0 -> x1, Pallas kernels: none -> 71.7 us  [per_device(): pl.pallas_call(functools.partial(kernel, side, feat_total), out_shape=(ja...]
    psum x1 -> x0, waiting for transfers between devices: 59.8 us -> none  [per_device(): sketch, right_side = lax.psum((partial_value, right_part), 'feat')]
    all_gather x1 -> x0, blocking collectives: 51.7 us -> none  [per_device(): values = lax.all_gather(owned_values, 'rows', axis=1, tiled=True)]
    dot_general x8 -> x0, matrix products: 17.4 us -> none  [the longest x4 12.2 us: one_group(): lax.dot_general(one_hot, weighted, (((2,), (0,)), ((), ())), preferred_el...]
    psum x1 -> x0, blocking collectives: 14.9 us -> none  [per_device(): sketch, right_side = lax.psum((partial_value, right_part), 'feat')]
    convert_element_type x6 -> x0, other arithmetic: 6.71 us -> none  [the longest x4 3.81 us: per_device(): weighted = (slot_mask.astype(jnp.float32)[:, :, None] * sketch[:, None, :...]
  transfers between devices with their start and end apart: 2 -> 0, of which waited for: 1 -> 0; matrix products, arithmetic and copies ran while one was open for 1% -> 0% of each run, Pallas kernels for 0% -> 0%
where the time goes in v1:
time: 81.6 us; the launch traced here: 81.3 us
  Pallas kernels  71.7 us (88%)
  local copies, waits for them, and re-layouts  8.92 us (11%)
    pallas_call x1, Pallas kernels, per_device(): pl.pallas_call(functools.partial(kernel, side, feat_total), out_shape=(ja...  71.7 us
    unnamed x16, local copies, waits for them, and re-layouts  8.22 us

profile of v1, /device:TPU:8, one launch (start us, length us, event | category | flops | bytes accessed | tf_op | source)
XLA Modules:
  0.0 81.3 jit_solution(12148336516081589398)
XLA Ops:
  0.6 0.7 reshape.7.node_ref
  1.3 0.0 copy-start
  1.3 1.4 %copy-done = bf16[1536,512]{1,0:T(8,128)(2,1)S(1)} copy-done((bf16[1536,512]{1,0:T(8,128)(2,1)S(1)}, bf16[1536,512]{1,0:T(8,128)(2,1)}, u32[]{:S(2)}) %copy-start) | copy-done | bytes 1572888
  2.7 0.0 copy-start.1
  2.7 1.4 %copy-done.1 = bf16[1536,512]{1,0:T(8,128)(2,1)S(1)} copy-done((bf16[1536,512]{1,0:T(8,128)(2,1)S(1)}, bf16[1536,512]{1,0:T(8,128)(2,1)}, u32[]{:S(2)}) %copy-start.1) | copy-done | bytes 1572888
  4.1 0.0 copy-start.2
  4.2 0.9 %copy-done.2 = s32[32,1536]{1,0:T(8,128)S(1)} copy-done((s32[32,1536]{1,0:T(8,128)S(1)}, s32[32,1536]{1,0:T(8,128)}, u32[]{:S(2)}) %copy-start.2) | copy-done | bytes 196632
  5.1 0.0 copy-start.3
  5.1 0.8 copy-done.3
  5.8 0.0 copy-start.4
  5.8 0.7 copy-done.4
  6.5 0.0 copy-start.5
  6.5 0.7 copy-done.5
  7.1 0.0 copy-start.6
  7.1 0.7 copy-done.6
  7.8 71.7 %boost.1 = (bf16[1536,512]{1,0:T(8,128)(2,1)S(1)}, f32[4,2048]{1,0:T(4,128)S(1)}) custom-call(bf16[1536,512]{1,0:T(8,128)(2,1)S(1)} %copy-done, bf16[1536,512]{1,0:T(8,128)(2,1)S(1)} %copy-done.1, bf16[32,512]{1,0:T(8,128)(2,1)S(1)} %copy-done.3, s32[32,1536]{1,0:T(8,128)S(1)} %copy-done.2, s32[1,1536]{1,0:T(1,128)S(1)} %reshape.7.node_ref, s32[4]{0:T(128)S(1)} %copy-done.4, ...), custom_call_target="tpu_custom_call" | custom-call | tf_op jit(solution)/shard_map/boost/pallas_call | solution.py:476
  79.5 1.1 %copy.12 = bf16[1536,512]{1,0:T(8,128)(2,1)} copy(bf16[1536,512]{1,0:T(8,128)(2,1)S(1)} %get-tuple-element.4) | data formatting | bytes 3145728
  80.7 0.6 copy.13
Async XLA Ops:
  1.3 1.4 %copy-start = (bf16[1536,512]{1,0:T(8,128)(2,1)S(1)}, bf16[1536,512]{1,0:T(8,128)(2,1)}, u32[]{:S(2)}) copy-start(bf16[1536,512]{1,0:T(8,128)(2,1)} %pred_hbm.1) | copy-start | bytes 4718596
  2.7 1.4 %copy-start.1 = (bf16[1536,512]{1,0:T(8,128)(2,1)S(1)}, bf16[1536,512]{1,0:T(8,128)(2,1)}, u32[]{:S(2)}) copy-start(bf16[1536,512]{1,0:T(8,128)(2,1)} %targ_hbm.1) | copy-start | bytes 4718596
  4.1 0.9 %copy-start.2 = (s32[32,1536]{1,0:T(8,128)S(1)}, s32[32,1536]{1,0:T(8,128)}, u32[]{:S(2)}) copy-start(s32[32,1536]{1,0:T(8,128)} %codes_ref.1) | copy-start | bytes 589828
  5.1 0.8 copy-start.3
  5.8 0.7 copy-start.4
  6.5 0.7 copy-start.5
  7.1 0.7 copy-start.6

commit v2 on v1

v2 whole, which is shorter than its diff:
```python
import functools
import math

import jax
import jax.numpy as jnp
from jax import lax
from jax.experimental import pallas as pl
from jax.experimental.pallas import tpu as pltpu
from jax.sharding import PartitionSpec as P

BINS = 256
DAMPING = 1.0
SHRINKAGE = 0.5
GROUP = 2
RINGS = 0
LOWER = 16.0
CHUNK = 256
BLOCK = 64
MESH = pl.DeviceIdType.MESH


def kernel(
    side,
    feat_total,
    pred_hbm,
    targ_hbm,
    matrix_hbm,
    codes_hbm,
    node_hbm,
    smaller_ref,
    feature_ref,
    bin_ref,
    newp,
    hist_ref,
    pred,
    targ,
    matrix,
    codes,
    node_line,
    grad,
    hess,
    part,
    part_in,
    sketch,
    right,
    right_in,
    weights,
    lines,
    bins,
    one_hots,
    hist,
    ring_in,
    last_out,
    last_in,
    leaf_out,
    leaf_in,
    leaf_sum,
    leaf_sum_in,
    value_own,
    value_in,
    values,
    leaf_hot,
    load_sem,
    small_sem,
    right_send,
    right_recv,
    part_send,
    part_recv,
    sketch_send,
    sketch_recv,
    ring_send,
    ring_recv,
    last_send,
    last_recv,
    leaf_send,
    leaf_recv,
):
    row_count, label_count = grad.shape
    chunks = row_count // CHUNK
    feats = codes.shape[0]
    nodes = smaller_ref.shape[0]
    leaves = 2 * nodes
    groups = hist.shape[0] // GROUP
    half = side // 2
    owned_bins = BINS // (side * side)
    ring_bins = BINS // side
    leaf_part = leaves // side

    here = lax.axis_index("rows")
    me_z = here // side
    me_y = here % side
    me_f = lax.axis_index("feat")
    me_of = (me_y, me_z)

    def at_y(k):
        return {"rows": me_z * side + (me_y + k + side) % side}

    def at_z(k):
        return {"rows": ((me_z + k + side) % side) * side + me_y}

    at_of = (at_y, at_z)

    def at_f(k):
        return {"feat": (me_f + k) % feat_total}

    def remote(src, dst, send, recv, where):
        return pltpu.make_async_remote_copy(
            src_ref=src,
            dst_ref=dst,
            send_sem=send,
            recv_sem=recv,
            device_id=where,
            device_id_type=MESH,
        )

    def loads(c):
        rows = pl.ds(c * CHUNK, CHUNK)
        return (
            pltpu.make_async_copy(pred_hbm.at[rows], pred.at[rows], load_sem.at[0, c]),
            pltpu.make_async_copy(targ_hbm.at[rows], targ.at[rows], load_sem.at[1, c]),
        )

    small_loads = (
        pltpu.make_async_copy(node_hbm, node_line, small_sem.at[0]),
        pltpu.make_async_copy(codes_hbm, codes, small_sem.at[1]),
        pltpu.make_async_copy(matrix_hbm, matrix, small_sem.at[2]),
    )
    barrier = pltpu.get_barrier_semaphore()
    for k in range(1, feat_total):
        pl.semaphore_signal(barrier, inc=1, device_id=at_f(k), device_id_type=MESH)
    for k in range(1, side):
        pl.semaphore_signal(barrier, inc=1, device_id=at_y(k), device_id_type=MESH)
        pl.semaphore_signal(barrier, inc=1, device_id=at_z(k), device_id_type=MESH)
    for copy in small_loads:
        copy.start()
    for c in range(chunks):
        for copy in loads(c):
            copy.start()

    place = lax.broadcasted_iota(jnp.int32, (BINS, 128), 0)
    major, rest = place // ring_bins, place % ring_bins
    minor, low = rest // owned_bins, rest % owned_bins
    bins[0] = ((minor * side + major) * owned_bins + low).astype(jnp.float32).astype(jnp.bfloat16)
    bins[1] = place.astype(jnp.float32).astype(jnp.bfloat16)
    for copy in small_loads:
        copy.wait()

    def elementwise(c):
        for copy in loads(c):
            copy.wait()

        def block(b, carry):
            rows = pl.ds(pl.multiple_of(c * CHUNK + b * BLOCK, BLOCK), BLOCK)
            logits = pred[rows, :].astype(jnp.float32)
            prob = 0.5 * jnp.tanh(0.5 * logits) + 0.5
            grad[rows, :] = (prob - targ[rows, :].astype(jnp.float32)).astype(jnp.bfloat16)
            hess[rows, :] = (prob * (1.0 - prob)).astype(jnp.bfloat16)
            return carry

        lax.fori_loop(0, CHUNK // BLOCK, block, 0)
        rows = pl.ds(c * CHUNK, CHUNK)
        part[:, rows] = lax.dot_general(
            matrix[...],
            grad[rows, :],
            (((1,), (1,)), ((), ())),
            preferred_element_type=jnp.float32,
        )

    for c in range(chunks):
        elementwise(c)

    node = jnp.concatenate(
        [node_line[pl.ds(i * 128, 128)].reshape(1, 128) for i in range(row_count // 128)], axis=1
    )
    right_part = jnp.zeros((1, row_count), jnp.float32)
    for n in range(nodes):
        local = feature_ref[n] - me_f * feats
        mine = (local >= 0) & (local < feats)
        row = codes[pl.ds(jnp.clip(local, 0, feats - 1), 1), :]
        limit = jnp.where(mine, bin_ref[n], BINS)
        right_part += jnp.where((node == n) & (row > limit), 1.0, 0.0)
    right[...] = right_part

    piece_rows, piece_lanes = part_in.shape[1:]
    lane_parts = row_count // piece_lanes

    def piece(f):
        return (
            pl.ds(pl.multiple_of((f // lane_parts) * piece_rows, piece_rows), piece_rows),
            pl.ds(pl.multiple_of((f % lane_parts) * piece_lanes, 128), piece_lanes),
        )

    def right_copy(k):
        return remote(right, right_in.at[k], right_send.at[k], right_recv.at[k], at_f(k))

    def part_copy(k):
        return remote(
            part.at[piece((me_f + k) % feat_total)],
            part_in.at[k],
            part_send.at[k],
            part_recv.at[k],
            at_f(k),
        )

    def sketch_copy(k, owner):
        return remote(
            sketch.at[piece(owner)],
            sketch.at[piece(owner)],
            sketch_send.at[k],
            sketch_recv.at[k],
            at_f(k),
        )

    lines[...] = codes[...].astype(jnp.float32)

    def build(first, last):
        def one(f, carry):
            turn = (f // (2 * GROUP)) % 2
            row = lines[pl.ds(f, 1), :]
            tile = jnp.broadcast_to(row, (16, row_count)).astype(jnp.bfloat16)
            wanted = jnp.concatenate([tile] * (BINS // 16), axis=0)
            ids = jnp.concatenate([bins[turn]] * (row_count // 128), axis=1)
            hot = jnp.where(ids == wanted, jnp.bfloat16(1), jnp.bfloat16(0))
            one_hots[f % 2, f // 2] = hot.astype(one_hots.dtype)
            return carry

        lax.fori_loop(first, last, one, 0)

    third = feats // 4
    build(0, third)
    pl.semaphore_wait(barrier, feat_total - 1 + 2 * (side - 1))
    for k in range(1, feat_total):
        part_copy(k).start()
    for k in range(1, feat_total):
        right_copy(k).start()
    build(third, 3 * third)

    mine = part[piece(me_f)]
    for k in range(1, feat_total):
        part_copy(k).wait()
        mine = mine + part_in[k]
    sketch[piece(me_f)] = mine
    for k in range(1, feat_total):
        sketch_copy(k, me_f).start()

    side_of = right_part
    for k in range(1, feat_total):
        right_copy(k).wait()
        side_of = side_of + right_in[k]
    leaf_id = 2 * node + (side_of > 0.5).astype(jnp.int32)
    tall = lax.broadcasted_iota(jnp.int32, (128, row_count), 0)
    hot = jnp.where((tall % leaves == leaf_id) & (tall < 3 * leaves), 1.0, 0.0)
    wide = hot[:leaves].astype(jnp.bfloat16)
    grad_sum = jnp.dot(wide, grad[...], preferred_element_type=jnp.float32)
    hess_sum = jnp.dot(wide, hess[...], preferred_element_type=jnp.float32)
    for i in range(side):
        leaf_out[i, :leaf_part, :] = grad_sum[i * leaf_part : (i + 1) * leaf_part]
        leaf_out[i, leaf_part:, :] = hess_sum[i * leaf_part : (i + 1) * leaf_part]

    def leaf_copy(k):
        return remote(
            leaf_out.at[(me_y + k) % side],
            leaf_in.at[k],
            leaf_send.at[0, k],
            leaf_recv.at[0, k],
            at_y(k),
        )

    def leaf_sum_copy(k):
        return remote(
            leaf_sum, leaf_sum_in.at[k], leaf_send.at[1, k], leaf_recv.at[1, k], at_z(k)
        )

    def value_copy(k):
        return remote(value_own, value_in.at[k], leaf_send.at[2, k], leaf_recv.at[2, k], at_y(k))

    for k in range(1, side):
        leaf_copy(k).start()
    leaf_hot[...] = hot.T.astype(jnp.bfloat16)
    build(3 * third, feats)

    for k in range(1, feat_total):
        sketch_copy(k, me_f).wait_send()
        sketch_copy(k, (me_f - k + feat_total) % feat_total).wait_recv()

    full = sketch[...]
    slots = []
    for s in range(nodes // 2):
        keep = jnp.zeros((1, row_count), jnp.float32)
        for n in (2 * s, 2 * s + 1):
            keep += jnp.where((node == n) & (smaller_ref[n] == 1), 1.0, 0.0)
        slots.append(full * keep)
    picked = jnp.concatenate(slots, axis=0).astype(jnp.bfloat16).astype(jnp.float32)
    most = jnp.max(jnp.abs(picked), axis=(0, 1), keepdims=True)
    power = jnp.floor(jnp.log2(jnp.maximum(most, 1e-30)))
    scaled = picked * jnp.exp2(7.0 - power)
    upper = scaled.astype(jnp.bfloat16).astype(weights.dtype).astype(jnp.float32)
    lower = (scaled - upper) * LOWER
    empty = jnp.zeros_like(picked)
    for i in (0, 1):
        for j, term in enumerate((upper, lower)):
            both = (term, empty) if i == 0 else (empty, term)
            turned = jnp.concatenate(both, axis=0).T.astype(jnp.bfloat16)
            weights[i, :, j * 128 : (j + 1) * 128] = turned.astype(weights.dtype)
    unscale = jnp.exp2(power - 7.0)

    def pairs_of(g):
        return pl.ds(g * GROUP, GROUP)

    def compute(g):
        total = None
        for i in (0, 1):
            left = one_hots[i, pairs_of(g)].reshape(GROUP * BINS, row_count)
            product = jnp.dot(left, weights[i], preferred_element_type=jnp.float32)
            total = product if total is None else total + product
        total = (total[:, :128] + total[:, 128:] * (1.0 / LOWER)) * unscale
        hist[pairs_of(g)] = total.reshape(GROUP, BINS, 128)

    def rows_of(target):
        return pl.ds(pl.multiple_of((target + side) % side * ring_bins, ring_bins), ring_bins)

    def ring_range(way, step):
        return (way * (GROUP // 2), GROUP // 2) if step == 0 else (0, GROUP)

    def ring_copy(g, way, step):
        sign = 1 - 2 * way
        start, count = ring_range(way, step)
        return remote(
            hist.at[
                pl.ds(g * GROUP + start, count),
                rows_of(me_of[g % 2] + sign * (half - step)),
            ],
            ring_in.at[g, way, step, pl.ds(start, count)],
            ring_send.at[g, way, step],
            ring_recv.at[g, way, step],
            at_of[g % 2](sign),
        )

    def ring_step(g, k):
        for way in (0, 1):
            if k > 0:
                ring_copy(g, way, k - 1).wait()
                start, count = ring_range(way, k - 1)
                spot = (
                    pl.ds(g * GROUP + start, count),
                    rows_of(me_of[g % 2] + (1 - 2 * way) * (half - k)),
                    slice(None),
                )
                hist[spot] = hist[spot] + ring_in[g, way, k - 1, start : start + count]
            if k < half:
                ring_copy(g, way, k).start()

    relay = max(1, half // 2)

    def relay_copy(g, way, d):
        sign = 1 - 2 * way
        start, count = ring_range(way, half - d)
        return remote(
            hist.at[pl.ds(g * GROUP + start, count), rows_of(me_of[g % 2] + sign * d)],
            ring_in.at[g, way, d - 1, pl.ds(start, count)],
            ring_send.at[g, way, d - 1],
            ring_recv.at[g, way, d - 1],
            at_of[g % 2](sign * (d - relay if d > relay else d)),
        )

    def relay_take(g, way, d, target):
        relay_copy(g, way, d).wait()
        start, count = ring_range(way, half - d)
        spot = (pl.ds(g * GROUP + start, count), rows_of(target), slice(None))
        hist[spot] = hist[spot] + ring_in[g, way, d - 1, start : start + count]

    def relay_start(g):
        for d in range(half, 0, -1):
            if d != relay or relay == half:
                for way in (0, 1):
                    relay_copy(g, way, d).start()

    def relay_pass(g):
        if relay < half:
            for way, sign in ((0, 1), (1, -1)):
                for d in range(half, relay, -1):
                    relay_take(g, way, d, me_of[g % 2] + sign * relay)
                relay_copy(g, way, relay).start()

    def relay_end(g):
        for d in range(1, relay + 1):
            for way in (0, 1):
                relay_take(g, way, d, me_of[g % 2])

    by_distance = sorted(range(1, side), key=lambda k: -min(k, side - k))

    def last_copy(g, k):
        return remote(
            last_out.at[g, (me_of[1 - g % 2] + k) % side],
            last_in.at[g, k],
            last_send.at[g, k],
            last_recv.at[g, k],
            at_of[1 - g % 2](k),
        )

    def finish(g):
        if g < RINGS:
            ring_step(g, half)
        else:
            relay_end(g)
        total = hist[pairs_of(g), rows_of(me_of[g % 2]), :]
        for i in range(side):
            last_out[g, i] = total[:, i * owned_bins : (i + 1) * owned_bins]
        for k in by_distance:
            last_copy(g, k).start()

    def collect(g):
        total = last_out[g, me_of[1 - g % 2]]
        for k in range(1, side):
            last_copy(g, k).wait()
            total = total + last_in[g, k]
        for i in range(GROUP):
            hist_ref[:, (g * GROUP + i) * 128 : (g * GROUP + i + 1) * 128] = total[i]

    def leaf_first():
        total = leaf_out[me_y]
        for k in range(1, side):
            leaf_copy(k).wait()
            total = total + leaf_in[k]
        leaf_sum[...] = total
        for k in range(1, side):
            leaf_sum_copy(k).start()

    def leaf_second():
        total = leaf_sum[...]
        for k in range(1, side):
            leaf_sum_copy(k).wait()
            total = total + leaf_sum_in[k]
        value_own[...] = -total[:leaf_part] / (total[leaf_part:] + DAMPING)
        for k in range(1, side):
            value_copy(k).start()

    def leaf_third():
        for k in range(1, side):
            value_copy(k).wait()
        who = lax.broadcasted_iota(jnp.int32, (leaves, label_count), 0) // leaf_part
        found = jnp.zeros((leaves, label_count), jnp.float32)
        for k in range(side):
            owner = (me_y - k + side) % side
            row = value_own[...] if k == 0 else value_in[k]
            tiled = jnp.concatenate([row] * side, axis=0)
            found = jnp.where(who == owner, tiled, found)
        high = found.astype(jnp.bfloat16).astype(jnp.float32)
        rest = found - high
        middle = rest.astype(jnp.bfloat16).astype(jnp.float32)
        pad = jnp.zeros((128 - 3 * leaves, label_count), jnp.float32)
        values[...] = jnp.concatenate([high, middle, rest - middle, pad], 0).astype(jnp.bfloat16)

    def update(c):
        rows = pl.ds(c * CHUNK, CHUNK)
        moved = jnp.dot(leaf_hot[rows, :], values[...], preferred_element_type=jnp.float32)
        newp[rows, :] = (pred[rows, :].astype(jnp.float32) + SHRINKAGE * moved).astype(
            jnp.bfloat16
        )

    plan = [(3.0, leaf_first), (8.5, leaf_second), (13.5, leaf_third)]
    for g in range(groups):
        compute(g)
        ready = 0.6 * (g + 1)
        if g < RINGS:
            ring_step(g, 0)
            for k in range(1, half):
                plan.append((ready + 3.6 * k, functools.partial(ring_step, g, k)))
            ready += 3.6 * half
        else:
            relay_start(g)
            plan.append((ready + 5.0, functools.partial(relay_pass, g)))
            ready += 10.0
        plan.append((ready, functools.partial(finish, g)))
        plan.append((max(ready, 18.0) + 6.0, functools.partial(collect, g)))
    for c in range(chunks):
        plan.append((23.9, functools.partial(update, c)))
    for _, step in sorted(plan, key=lambda item: item[0]):
        step()


def per_device(
    side,
    feat_total,
    predictions,
    targets,
    sketch_matrix,
    bin_codes,
    row_node,
    smaller,
    split_feature,
    split_bin,
):
    row_count, label_count = predictions.shape
    columns = sketch_matrix.shape[0]
    feats = bin_codes.shape[0]
    pairs = feats // 2
    groups = pairs // GROUP
    half = side // 2
    owned_bins = BINS // (side * side)
    leaves = 2 * smaller.shape[0]
    leaf_part = leaves // side
    chunks = row_count // CHUNK
    lane_parts = max(1, feat_total * 8 // columns)
    piece = (columns * lane_parts // feat_total, row_count // lane_parts)
    vmem = pltpu.VMEM
    bf16, f32, i32, f8 = jnp.bfloat16, jnp.float32, jnp.int32, jnp.float8_e4m3fn
    dma = pltpu.SemaphoreType.DMA
    whole = pl.BlockSpec(memory_space=pltpu.VMEM)
    scalar = pl.BlockSpec(memory_space=pltpu.SMEM)
    far = pl.BlockSpec(memory_space=pltpu.HBM)
    wide_shape = (row_count, label_count)
    return pl.pallas_call(
        functools.partial(kernel, side, feat_total),
        out_shape=(
            jax.ShapeDtypeStruct(wide_shape, bf16),
            jax.ShapeDtypeStruct((owned_bins, pairs * 128), f32),
        ),
        in_specs=[far] * 5 + [scalar] * 3,
        out_specs=(whole, whole),
        scratch_shapes=[
            vmem(wide_shape, bf16),
            vmem(wide_shape, bf16),
            vmem((columns, label_count), bf16),
            vmem((feats, row_count), i32),
            vmem((row_count,), i32),
            vmem(wide_shape, bf16),
            vmem(wide_shape, bf16),
            vmem((columns, row_count), f32),
            vmem((feat_total,) + piece, f32),
            vmem((columns, row_count), f32),
            vmem((1, row_count), f32),
            vmem((feat_total, 1, row_count), f32),
            vmem((2, row_count, 256), f8),
            vmem((feats, row_count), f32),
            vmem((2, BINS, 128), bf16),
            vmem((2, pairs, BINS, row_count), f8),
            vmem((pairs, BINS, 128), f32),
            vmem((groups, 2, half, GROUP, BINS // side, 128), f32),
            vmem((groups, side, GROUP, owned_bins, 128), f32),
            vmem((groups, side, GROUP, owned_bins, 128), f32),
            vmem((side, 2 * leaf_part, label_count), f32),
            vmem((side, 2 * leaf_part, label_count), f32),
            vmem((2 * leaf_part, label_count), f32),
            vmem((side, 2 * leaf_part, label_count), f32),
            vmem((leaf_part, label_count), f32),
            vmem((side, leaf_part, label_count), f32),
            vmem((128, label_count), bf16),
            vmem((row_count, 128), bf16),
            dma((2, chunks)),
            dma((3,)),
            dma((feat_total,)),
            dma((feat_total,)),
            dma((feat_total,)),
            dma((feat_total,)),
            dma((feat_total,)),
            dma((feat_total,)),
            dma((groups, 2, half)),
            dma((groups, 2, half)),
            dma((groups, side)),
            dma((groups, side)),
            dma((3, side)),
            dma((3, side)),
        ],
        compiler_params=pltpu.CompilerParams(
            collective_id=0, has_side_effects=True, vmem_limit_bytes=62 << 20
        ),
        name="boost",
    )(
        predictions,
        targets,
        sketch_matrix,
        bin_codes,
        row_node,
        smaller,
        split_feature,
        split_bin,
    )


def solution(mesh):
    placed = (
        P("rows", "feat"),
        P("rows", "feat"),
        P(None, "feat"),
        P("feat", "rows"),
        P("rows"),
        P(),
        P(),
        P(),
    )
    side = math.isqrt(mesh.shape["rows"])
    return jax.shard_map(
        functools.partial(per_device, side, mesh.shape["feat"]),
        mesh=mesh,
        in_specs=placed,
        out_specs=(P("rows", "feat"), P("rows", "feat")),
        check_vma=False,
    )
```

time: 81.6 us -> 60 us (0.74)
  the two profiles are of different devices: /device:TPU:8 before, /device:TPU:64 now
where the time goes in v2:
time: 60 us; the launch traced here: 59.9 us
  Pallas kernels  56 us (93%)
  local copies, waits for them, and re-layouts  3.28 us (5%)
  between operations  0.65 us (1%)
    pallas_call x1, Pallas kernels, per_device(): pl.pallas_call(functools.partial(kernel, side, feat_total), out_shape=(ja...  56 us
    unnamed x4, local copies, waits for them, and re-layouts  3.28 us

profile of v2, /device:TPU:64, one launch (start us, length us, event | category | flops | bytes accessed | tf_op | source)
XLA Modules:
  0.0 59.9 jit_solution(9044168299550814797)
XLA Ops:
  0.6 56.0 %boost.1 = (bf16[1536,512]{1,0:T(8,128)(2,1)}, f32[4,2048]{1,0:T(4,128)}) custom-call(bf16[1536,512]{1,0:T(8,128)(2,1)} %pred_hbm.1, bf16[1536,512]{1,0:T(8,128)(2,1)} %targ_hbm.1, bf16[32,512]{1,0:T(8,128)(2,1)} %matrix_hbm.1, s32[32,1536]{1,0:T(8,128)} %codes_hbm.1, s32[1536]{0:T(1024)} %node_hbm.1, s32[4]{0:T(128)} %smaller_ref.1, s32[4]{0:T(128)} %feature_ref.1, ...), custom_call_target="tpu_custom_call" | custom-call | tf_op jit(solution)/shard_map/boost/pallas_call | solution.py:513
  56.6 0.0 copy-start
  56.6 2.7 %copy.12 = bf16[1536,512]{1,0:T(8,128)(2,1)} copy(bf16[1536,512]{1,0:T(8,128)(2,1)} %get-tuple-element.4) | data formatting | bytes 3145728
  59.3 0.0 copy-done
  59.3 0.6 %copy.13 = f32[4,2048]{1,0:T(4,128)} copy(f32[4,2048]{1,0:T(4,128)S(1)} %copy-done) | data formatting | bytes 65536
Async XLA Ops:
  56.6 2.7 %copy-start = (f32[4,2048]{1,0:T(4,128)S(1)}, f32[4,2048]{1,0:T(4,128)}, u32[]{:S(2)}) copy-start(f32[4,2048]{1,0:T(4,128)} %get-tuple-element.5) | copy-start | bytes 98308

commit v3 on v2

--- a/solution.py
+++ b/solution.py
@@ -11,8 +11,9 @@
 BINS = 256
 DAMPING = 1.0
 SHRINKAGE = 0.5
-GROUP = 2
-RINGS = 0
+UNIT = 2
+GROUPS = ((0, 0, 2), (1, 0, 2), (0, 2, 4), (1, 2, 4), (0, 6, 2), (1, 6, 2))
+WIDEST = 4
 LOWER = 16.0
 CHUNK = 256
 BLOCK = 64
@@ -30,7 +31,7 @@
     smaller_ref,
     feature_ref,
     bin_ref,
-    newp,
+    newp_hbm,
     hist_ref,
     pred,
     targ,
@@ -60,8 +61,10 @@
     value_in,
     values,
     leaf_hot,
+    newp,
     load_sem,
     small_sem,
+    store_sem,
     right_send,
     right_recv,
     part_send,
@@ -80,7 +83,7 @@
     feats = codes.shape[0]
     nodes = smaller_ref.shape[0]
     leaves = 2 * nodes
-    groups = hist.shape[0] // GROUP
+    per_axis = hist.shape[0] // 2
     half = side // 2
     owned_bins = BINS // (side * side)
     ring_bins = BINS // side
@@ -215,13 +218,15 @@
 
     def build(first, last):
         def one(f, carry):
-            turn = (f // (2 * GROUP)) % 2
+            unit = f // (2 * UNIT)
+            turn = unit % 2
+            slot = turn * per_axis + unit // 2 * UNIT + f // 2 % UNIT
             row = lines[pl.ds(f, 1), :]
             tile = jnp.broadcast_to(row, (16, row_count)).astype(jnp.bfloat16)
             wanted = jnp.concatenate([tile] * (BINS // 16), axis=0)
             ids = jnp.concatenate([bins[turn]] * (row_count // 128), axis=1)
             hot = jnp.where(ids == wanted, jnp.bfloat16(1), jnp.bfloat16(0))
-            one_hots[f % 2, f // 2] = hot.astype(one_hots.dtype)
+            one_hots[f % 2, slot] = hot.astype(one_hots.dtype)
             return carry
 
         lax.fori_loop(first, last, one, 0)
@@ -296,77 +301,59 @@
     scaled = picked * jnp.exp2(7.0 - power)
     upper = scaled.astype(jnp.bfloat16).astype(weights.dtype).astype(jnp.float32)
     lower = (scaled - upper) * LOWER
-    empty = jnp.zeros_like(picked)
+    turned = jnp.concatenate([upper, lower], axis=0).T
+    swapped = pltpu.roll(turned, 64, 1)
+    left_half = lax.broadcasted_iota(jnp.int32, turned.shape, 1) < 64
+    tables = (
+        (jnp.where(left_half, turned, 0.0), jnp.where(left_half, swapped, 0.0)),
+        (jnp.where(left_half, 0.0, swapped), jnp.where(left_half, 0.0, turned)),
+    )
     for i in (0, 1):
-        for j, term in enumerate((upper, lower)):
-            both = (term, empty) if i == 0 else (empty, term)
-            turned = jnp.concatenate(both, axis=0).T.astype(jnp.bfloat16)
-            weights[i, :, j * 128 : (j + 1) * 128] = turned.astype(weights.dtype)
+        for j in (0, 1):
+            table = tables[i][j].astype(jnp.bfloat16)
+            weights[i, :, j * 128 : (j + 1) * 128] = table.astype(weights.dtype)
     unscale = jnp.exp2(power - 7.0)
 
+    axis_of = [axis for axis, _, _ in GROUPS]
+    size_of = [size for _, _, size in GROUPS]
+    start_of = [axis * per_axis + first for axis, first, _ in GROUPS]
+
     def pairs_of(g):
-        return pl.ds(g * GROUP, GROUP)
+        return pl.ds(start_of[g], size_of[g])
 
     def compute(g):
         total = None
         for i in (0, 1):
-            left = one_hots[i, pairs_of(g)].reshape(GROUP * BINS, row_count)
+            left = one_hots[i, pairs_of(g)].reshape(size_of[g] * BINS, row_count)
             product = jnp.dot(left, weights[i], preferred_element_type=jnp.float32)
             total = product if total is None else total + product
         total = (total[:, :128] + total[:, 128:] * (1.0 / LOWER)) * unscale
-        hist[pairs_of(g)] = total.reshape(GROUP, BINS, 128)
+        hist[pairs_of(g)] = total.reshape(size_of[g], BINS, 128)
 
     def rows_of(target):
         return pl.ds(pl.multiple_of((target + side) % side * ring_bins, ring_bins), ring_bins)
 
-    def ring_range(way, step):
-        return (way * (GROUP // 2), GROUP // 2) if step == 0 else (0, GROUP)
-
-    def ring_copy(g, way, step):
-        sign = 1 - 2 * way
-        start, count = ring_range(way, step)
-        return remote(
-            hist.at[
-                pl.ds(g * GROUP + start, count),
-                rows_of(me_of[g % 2] + sign * (half - step)),
-            ],
-            ring_in.at[g, way, step, pl.ds(start, count)],
-            ring_send.at[g, way, step],
-            ring_recv.at[g, way, step],
-            at_of[g % 2](sign),
-        )
-
-    def ring_step(g, k):
-        for way in (0, 1):
-            if k > 0:
-                ring_copy(g, way, k - 1).wait()
-                start, count = ring_range(way, k - 1)
-                spot = (
-                    pl.ds(g * GROUP + start, count),
-                    rows_of(me_of[g % 2] + (1 - 2 * way) * (half - k)),
-                    slice(None),
-                )
-                hist[spot] = hist[spot] + ring_in[g, way, k - 1, start : start + count]
-            if k < half:
-                ring_copy(g, way, k).start()
+    def pair_range(g, way, d):
+        size = size_of[g]
+        return (way * (size // 2), size // 2) if d == half else (0, size)
 
     relay = max(1, half // 2)
 
     def relay_copy(g, way, d):
         sign = 1 - 2 * way
-        start, count = ring_range(way, half - d)
+        start, count = pair_range(g, way, d)
         return remote(
-            hist.at[pl.ds(g * GROUP + start, count), rows_of(me_of[g % 2] + sign * d)],
+            hist.at[pl.ds(start_of[g] + start, count), rows_of(me_of[axis_of[g]] + sign * d)],
             ring_in.at[g, way, d - 1, pl.ds(start, count)],
             ring_send.at[g, way, d - 1],
             ring_recv.at[g, way, d - 1],
-            at_of[g % 2](sign * (d - relay if d > relay else d)),
+            at_of[axis_of[g]](sign * (d - relay if d > relay else d)),
         )
 
     def relay_take(g, way, d, target):
         relay_copy(g, way, d).wait()
-        start, count = ring_range(way, half - d)
-        spot = (pl.ds(g * GROUP + start, count), rows_of(target), slice(None))
+        start, count = pair_range(g, way, d)
+        spot = (pl.ds(start_of[g] + start, count), rows_of(target), slice(None))
         hist[spot] = hist[spot] + ring_in[g, way, d - 1, start : start + count]
 
     def relay_start(g):
@@ -379,43 +366,44 @@
         if relay < half:
             for way, sign in ((0, 1), (1, -1)):
                 for d in range(half, relay, -1):
-                    relay_take(g, way, d, me_of[g % 2] + sign * relay)
+                    relay_take(g, way, d, me_of[axis_of[g]] + sign * relay)
                 relay_copy(g, way, relay).start()
 
     def relay_end(g):
         for d in range(1, relay + 1):
             for way in (0, 1):
-                relay_take(g, way, d, me_of[g % 2])
+                relay_take(g, way, d, me_of[axis_of[g]])
 
     by_distance = sorted(range(1, side), key=lambda k: -min(k, side - k))
 
-    def last_copy(g, k):
+    def last_copy(c, k):
         return remote(
-            last_out.at[g, (me_of[1 - g % 2] + k) % side],
-            last_in.at[g, k],
-            last_send.at[g, k],
-            last_recv.at[g, k],
-            at_of[1 - g % 2](k),
+            last_out.at[c, (me_of[1 - c] + k) % side],
+            last_in.at[c, k],
+            last_send.at[c, k],
+            last_recv.at[c, k],
+            at_of[1 - c](k),
         )
 
     def finish(g):
-        if g < RINGS:
-            ring_step(g, half)
-        else:
-            relay_end(g)
-        total = hist[pairs_of(g), rows_of(me_of[g % 2]), :]
+        relay_end(g)
+        total = hist[pairs_of(g), rows_of(me_of[axis_of[g]]), :]
+        spot = pl.ds(GROUPS[g][1], size_of[g])
         for i in range(side):
-            last_out[g, i] = total[:, i * owned_bins : (i + 1) * owned_bins]
+            last_out[axis_of[g], i, spot] = total[:, i * owned_bins : (i + 1) * owned_bins]
+
+    def last_start(c):
         for k in by_distance:
-            last_copy(g, k).start()
-
-    def collect(g):
-        total = last_out[g, me_of[1 - g % 2]]
+            last_copy(c, k).start()
+
+    def collect(c):
+        total = last_out[c, me_of[1 - c]]
         for k in range(1, side):
-            last_copy(g, k).wait()
-            total = total + last_in[g, k]
-        for i in range(GROUP):
-            hist_ref[:, (g * GROUP + i) * 128 : (g * GROUP + i + 1) * 128] = total[i]
+            last_copy(c, k).wait()
+            total = total + last_in[c, k]
+        for i in range(total.shape[0]):
+            pair = (i // UNIT * 2 + c) * UNIT + i % UNIT
+            hist_ref[:, pair * 128 : (pair + 1) * 128] = total[i]
 
     def leaf_first():
         total = leaf_out[me_y]
@@ -451,32 +439,57 @@
         pad = jnp.zeros((128 - 3 * leaves, label_count), jnp.float32)
         values[...] = jnp.concatenate([high, middle, rest - middle, pad], 0).astype(jnp.bfloat16)
 
+    def stored(c):
+        rows = pl.ds(c * CHUNK, CHUNK)
+        return pltpu.make_async_copy(newp.at[rows], newp_hbm.at[rows], store_sem.at[c])
+
     def update(c):
         rows = pl.ds(c * CHUNK, CHUNK)
         moved = jnp.dot(leaf_hot[rows, :], values[...], preferred_element_type=jnp.float32)
         newp[rows, :] = (pred[rows, :].astype(jnp.float32) + SHRINKAGE * moved).astype(
             jnp.bfloat16
         )
-
-    plan = [(3.0, leaf_first), (8.5, leaf_second), (13.5, leaf_third)]
+        stored(c).start()
+
+    groups = len(GROUPS)
     for g in range(groups):
         compute(g)
-        ready = 0.6 * (g + 1)
-        if g < RINGS:
-            ring_step(g, 0)
-            for k in range(1, half):
-                plan.append((ready + 3.6 * k, functools.partial(ring_step, g, k)))
-            ready += 3.6 * half
-        else:
-            relay_start(g)
-            plan.append((ready + 5.0, functools.partial(relay_pass, g)))
-            ready += 10.0
-        plan.append((ready, functools.partial(finish, g)))
-        plan.append((max(ready, 18.0) + 6.0, functools.partial(collect, g)))
+        relay_start(g)
+        if g == 2:
+            leaf_first()
+    for g in range(groups):
+        relay_pass(g)
+    leaf_second()
+    for g in range(groups):
+        finish(g)
+        if g >= groups - 2:
+            last_start(axis_of[g])
+    leaf_third()
     for c in range(chunks):
-        plan.append((23.9, functools.partial(update, c)))
-    for _, step in sorted(plan, key=lambda item: item[0]):
-        step()
+        update(c)
+    for g in range(groups - 2, groups):
+        collect(axis_of[g])
+    for c in range(chunks):
+        stored(c).wait()
+
+
+def copy_kernel(newp_in, hist_in, newp_out, hist_out, newp, hist, in_sem, out_sem):
+    parts = in_sem.shape[0] - 1
+    size = newp.shape[0] // parts
+    moves = []
+    for i in range(parts):
+        rows = pl.ds(i * size, size)
+        moves.append((newp_in.at[rows], newp.at[rows], newp_out.at[rows]))
+    moves.append((hist_in, hist, hist_out))
+    ins = [pltpu.make_async_copy(a, b, in_sem.at[i]) for i, (a, b, c) in enumerate(moves)]
+    outs = [pltpu.make_async_copy(b, c, out_sem.at[i]) for i, (a, b, c) in enumerate(moves)]
+    for copy in ins:
+        copy.start()
+    for come, go in zip(ins, outs):
+        come.wait()
+        go.start()
+    for copy in outs:
+        copy.wait()
 
 
 def per_device(
@@ -495,7 +508,7 @@
     columns = sketch_matrix.shape[0]
     feats = bin_codes.shape[0]
     pairs = feats // 2
-    groups = pairs // GROUP
+    groups = len(GROUPS)
     half = side // 2
     owned_bins = BINS // (side * side)
     leaves = 2 * smaller.shape[0]
@@ -510,14 +523,14 @@
     scalar = pl.BlockSpec(memory_space=pltpu.SMEM)
     far = pl.BlockSpec(memory_space=pltpu.HBM)
     wide_shape = (row_count, label_count)
-    return pl.pallas_call(
+    newp, histograms = pl.pallas_call(
         functools.partial(kernel, side, feat_total),
         out_shape=(
             jax.ShapeDtypeStruct(wide_shape, bf16),
             jax.ShapeDtypeStruct((owned_bins, pairs * 128), f32),
         ),
         in_specs=[far] * 5 + [scalar] * 3,
-        out_specs=(whole, whole),
+        out_specs=(far, whole),
         scratch_shapes=[
             vmem(wide_shape, bf16),
             vmem(wide_shape, bf16),
@@ -536,9 +549,9 @@
             vmem((2, BINS, 128), bf16),
             vmem((2, pairs, BINS, row_count), f8),
             vmem((pairs, BINS, 128), f32),
-            vmem((groups, 2, half, GROUP, BINS // side, 128), f32),
-            vmem((groups, side, GROUP, owned_bins, 128), f32),
-            vmem((groups, side, GROUP, owned_bins, 128), f32),
+            vmem((groups, 2, half, WIDEST, BINS // side, 128), f32),
+            vmem((2, side, pairs // 2, owned_bins, 128), f32),
+            vmem((2, side, pairs // 2, owned_bins, 128), f32),
             vmem((side, 2 * leaf_part, label_count), f32),
             vmem((side, 2 * leaf_part, label_count), f32),
             vmem((2 * leaf_part, label_count), f32),
@@ -547,8 +560,10 @@
             vmem((side, leaf_part, label_count), f32),
             vmem((128, label_count), bf16),
             vmem((row_count, 128), bf16),
+            vmem(wide_shape, bf16),
             dma((2, chunks)),
             dma((3,)),
+            dma((chunks,)),
             dma((feat_total,)),
             dma((feat_total,)),
             dma((feat_total,)),
@@ -557,8 +572,8 @@
             dma((feat_total,)),
             dma((groups, 2, half)),
             dma((groups, 2, half)),
-            dma((groups, side)),
-            dma((groups, side)),
+            dma((2, side)),
+            dma((2, side)),
             dma((3, side)),
             dma((3, side)),
         ],
@@ -576,6 +591,23 @@
         split_feature,
         split_bin,
     )
+    return pl.pallas_call(
+        copy_kernel,
+        out_shape=(
+            jax.ShapeDtypeStruct(newp.shape, newp.dtype),
+            jax.ShapeDtypeStruct(histograms.shape, histograms.dtype),
+        ),
+        in_specs=[far, far],
+        out_specs=(far, far),
+        scratch_shapes=[
+            vmem(newp.shape, newp.dtype),
+            vmem(histograms.shape, histograms.dtype),
+            dma((chunks + 1,)),
+            dma((chunks + 1,)),
+        ],
+        compiler_params=pltpu.CompilerParams(vmem_limit_bytes=62 << 20),
+        name="hand_on",
+    )(newp, histograms)
 
 
 def solution(mesh):

time: 60 us -> 57.9 us (0.965)
  the two profiles are of different devices: /device:TPU:64 before, /device:TPU:8 now
where the time goes in v3:
time: 57.9 us; the launch traced here: 57.5 us
  Pallas kernels  56.9 us (98%)
  between operations  0.64 us (1%)
    pallas_call x1, Pallas kernels, per_device(): pl.pallas_call(functools.partial(kernel, side, feat_total), out_shape=(ja...  54.7 us
    pallas_call x1, Pallas kernels, per_device(): pl.pallas_call(copy_kernel, out_shape=(jax.ShapeDtypeStruct(newp.shape, n...  2.21 us

profile of v3, /device:TPU:8, one launch (start us, length us, event | category | flops | bytes accessed | tf_op | source)
XLA Modules:
  0.0 57.5 jit_solution(10723862547016631204)
XLA Ops:
  0.6 54.7 %boost.1 = (bf16[1536,512]{1,0:T(8,128)(2,1)}, f32[4,2048]{1,0:T(4,128)}) custom-call(bf16[1536,512]{1,0:T(8,128)(2,1)} %pred_hbm.1, bf16[1536,512]{1,0:T(8,128)(2,1)} %targ_hbm.1, bf16[32,512]{1,0:T(8,128)(2,1)} %matrix_hbm.1, s32[32,1536]{1,0:T(8,128)} %codes_hbm.1, s32[1536]{0:T(1024)} %node_hbm.1, s32[4]{0:T(128)} %smaller_ref.1, s32[4]{0:T(128)} %feature_ref.1, ...), custom_call_target="tpu_custom_call" | custom-call | tf_op jit(solution)/shard_map/boost/pallas_call | solution.py:526
  55.3 2.2 %hand_on.1 = (bf16[1536,512]{1,0:T(8,128)(2,1)}, f32[4,2048]{1,0:T(4,128)}) custom-call(bf16[1536,512]{1,0:T(8,128)(2,1)} %get-tuple-element.4.newp_in, f32[4,2048]{1,0:T(4,128)} %get-tuple-element.5.hist_in), custom_call_target="tpu_custom_call" | custom-call | tf_op jit(solution)/shard_map/hand_on/pallas_call | solution.py:594

commit v4 on v3

--- a/solution.py
+++ b/solution.py
@@ -13,7 +13,9 @@
 SHRINKAGE = 0.5
 UNIT = 2
 GROUPS = ((0, 0, 2), (1, 0, 2), (0, 2, 4), (1, 2, 4), (0, 6, 2), (1, 6, 2))
+CHAINED = (0, 1, 2, 3)
 WIDEST = 4
+ROUNDS = ((0, 6), (6, 2))
 LOWER = 16.0
 CHUNK = 256
 BLOCK = 64
@@ -339,6 +341,14 @@
 
     relay = max(1, half // 2)
 
+    def chained(g):
+        return g in CHAINED and 1 < relay < half
+
+    def hops(g, d):
+        if d > relay:
+            return d - relay
+        return d - 1 if chained(g) and d == relay and d > 1 else d
+
     def relay_copy(g, way, d):
         sign = 1 - 2 * way
         start, count = pair_range(g, way, d)
@@ -347,7 +357,7 @@
             ring_in.at[g, way, d - 1, pl.ds(start, count)],
             ring_send.at[g, way, d - 1],
             ring_recv.at[g, way, d - 1],
-            at_of[axis_of[g]](sign * (d - relay if d > relay else d)),
+            at_of[axis_of[g]](sign * hops(g, d)),
         )
 
     def relay_take(g, way, d, target):
@@ -358,7 +368,7 @@
 
     def relay_start(g):
         for d in range(half, 0, -1):
-            if d != relay or relay == half:
+            if (d > relay if chained(g) else d != relay) or relay == half:
                 for way in (0, 1):
                     relay_copy(g, way, d).start()
 
@@ -369,19 +379,26 @@
                     relay_take(g, way, d, me_of[axis_of[g]] + sign * relay)
                 relay_copy(g, way, relay).start()
 
+    def chain_pass(g):
+        if chained(g):
+            for way, sign in ((0, 1), (1, -1)):
+                relay_take(g, way, relay, me_of[axis_of[g]] + sign * (relay - 1))
+                relay_copy(g, way, relay - 1).start()
+
     def relay_end(g):
-        for d in range(1, relay + 1):
+        for d in range(1, relay if chained(g) else relay + 1):
             for way in (0, 1):
                 relay_take(g, way, d, me_of[axis_of[g]])
 
     by_distance = sorted(range(1, side), key=lambda k: -min(k, side - k))
 
-    def last_copy(c, k):
+    def last_copy(c, part, k):
+        spot = pl.ds(*ROUNDS[part])
         return remote(
-            last_out.at[c, (me_of[1 - c] + k) % side],
-            last_in.at[c, k],
-            last_send.at[c, k],
-            last_recv.at[c, k],
+            last_out.at[c, (me_of[1 - c] + k) % side, spot],
+            last_in.at[c, k, spot],
+            last_send.at[c, part, k],
+            last_recv.at[c, part, k],
             at_of[1 - c](k),
         )
 
@@ -392,18 +409,19 @@
         for i in range(side):
             last_out[axis_of[g], i, spot] = total[:, i * owned_bins : (i + 1) * owned_bins]
 
-    def last_start(c):
+    def last_start(c, part):
         for k in by_distance:
-            last_copy(c, k).start()
-
-    def collect(c):
-        total = last_out[c, me_of[1 - c]]
+            last_copy(c, part, k).start()
+
+    def collect(c, part):
+        first, count = ROUNDS[part]
+        total = last_out[c, me_of[1 - c], first : first + count]
         for k in range(1, side):
-            last_copy(c, k).wait()
-            total = total + last_in[c, k]
-        for i in range(total.shape[0]):
+            last_copy(c, part, k).wait()
+            total = total + last_in[c, k, first : first + count]
+        for i in range(first, first + count):
             pair = (i // UNIT * 2 + c) * UNIT + i % UNIT
-            hist_ref[:, pair * 128 : (pair + 1) * 128] = total[i]
+            hist_ref[:, pair * 128 : (pair + 1) * 128] = total[i - first]
 
     def leaf_first():
         total = leaf_out[me_y]
@@ -457,18 +475,27 @@
         relay_start(g)
         if g == 2:
             leaf_first()
-    for g in range(groups):
-        relay_pass(g)
+    relay_pass(0)
+    relay_pass(1)
+    relay_pass(2)
+    relay_pass(3)
+    chain_pass(0)
+    chain_pass(1)
+    relay_pass(4)
+    relay_pass(5)
     leaf_second()
+    chain_pass(2)
+    chain_pass(3)
     for g in range(groups):
         finish(g)
-        if g >= groups - 2:
-            last_start(axis_of[g])
+        if g >= groups - 4:
+            last_start(axis_of[g], (g - groups + 4) // 2)
     leaf_third()
     for c in range(chunks):
         update(c)
-    for g in range(groups - 2, groups):
-        collect(axis_of[g])
+    for part in range(2):
+        for c in (0, 1):
+            collect(c, part)
     for c in range(chunks):
         stored(c).wait()
 
@@ -572,8 +599,8 @@
             dma((feat_total,)),
             dma((groups, 2, half)),
             dma((groups, 2, half)),
-            dma((2, side)),
-            dma((2, side)),
+            dma((2, len(ROUNDS), side)),
+            dma((2, len(ROUNDS), side)),
             dma((3, side)),
             dma((3, side)),
         ],

time: 57.9 us -> 57.6 us (level)
  no operation moved by 1% of the time
where the time goes in v4:
time: 57.6 us; the launch traced here: 57.4 us
  Pallas kernels  56.7 us (98%)
  between operations  0.64 us (1%)
    pallas_call x1, Pallas kernels, per_device(): pl.pallas_call(functools.partial(kernel, side, feat_total), out_shape=(ja...  54.5 us
    pallas_call x1, Pallas kernels, per_device(): pl.pallas_call(copy_kernel, out_shape=(jax.ShapeDtypeStruct(newp.shape, n...  2.21 us

profile of v4, /device:TPU:8, one launch (start us, length us, event | category | flops | bytes accessed | tf_op | source)
XLA Modules:
  0.0 57.4 jit_solution(10795765525082672442)
XLA Ops:
  0.6 54.5 %boost.1 = (bf16[1536,512]{1,0:T(8,128)(2,1)}, f32[4,2048]{1,0:T(4,128)}) custom-call(bf16[1536,512]{1,0:T(8,128)(2,1)} %pred_hbm.1, bf16[1536,512]{1,0:T(8,128)(2,1)} %targ_hbm.1, bf16[32,512]{1,0:T(8,128)(2,1)} %matrix_hbm.1, s32[32,1536]{1,0:T(8,128)} %codes_hbm.1, s32[1536]{0:T(1024)} %node_hbm.1, s32[4]{0:T(128)} %smaller_ref.1, s32[4]{0:T(128)} %feature_ref.1, ...), custom_call_target="tpu_custom_call" | custom-call | tf_op jit(solution)/shard_map/boost/pallas_call | solution.py:553
  55.2 2.2 %hand_on.1 = (bf16[1536,512]{1,0:T(8,128)(2,1)}, f32[4,2048]{1,0:T(4,128)}) custom-call(bf16[1536,512]{1,0:T(8,128)(2,1)} %get-tuple-element.4.newp_in, f32[4,2048]{1,0:T(4,128)} %get-tuple-element.5.hist_in), custom_call_target="tpu_custom_call" | custom-call | tf_op jit(solution)/shard_map/hand_on/pallas_call | solution.py:621

commit v5 on v4

--- a/solution.py
+++ b/solution.py
@@ -131,11 +131,13 @@
         pltpu.make_async_copy(matrix_hbm, matrix, small_sem.at[2]),
     )
     barrier = pltpu.get_barrier_semaphore()
-    for k in range(1, feat_total):
-        pl.semaphore_signal(barrier, inc=1, device_id=at_f(k), device_id_type=MESH)
-    for k in range(1, side):
+    by_distance = sorted(range(1, side), key=lambda k: -min(k, side - k))
+    feat_order = sorted(range(1, feat_total), key=lambda k: -min(k, feat_total - k))
+    for k in by_distance:
         pl.semaphore_signal(barrier, inc=1, device_id=at_y(k), device_id_type=MESH)
         pl.semaphore_signal(barrier, inc=1, device_id=at_z(k), device_id_type=MESH)
+    for k in feat_order:
+        pl.semaphore_signal(barrier, inc=1, device_id=at_f(k), device_id_type=MESH)
     for copy in small_loads:
         copy.start()
     for c in range(chunks):
@@ -236,7 +238,7 @@
     third = feats // 4
     build(0, third)
     pl.semaphore_wait(barrier, feat_total - 1 + 2 * (side - 1))
-    for k in range(1, feat_total):
+    for k in feat_order:
         part_copy(k).start()
     for k in range(1, feat_total):
         right_copy(k).start()
@@ -247,7 +249,7 @@
         part_copy(k).wait()
         mine = mine + part_in[k]
     sketch[piece(me_f)] = mine
-    for k in range(1, feat_total):
+    for k in feat_order:
         sketch_copy(k, me_f).start()
 
     side_of = right_part
@@ -281,7 +283,7 @@
     def value_copy(k):
         return remote(value_own, value_in.at[k], leaf_send.at[2, k], leaf_recv.at[2, k], at_y(k))
 
-    for k in range(1, side):
+    for k in by_distance:
         leaf_copy(k).start()
     leaf_hot[...] = hot.T.astype(jnp.bfloat16)
     build(3 * third, feats)
@@ -390,8 +392,6 @@
             for way in (0, 1):
                 relay_take(g, way, d, me_of[axis_of[g]])
 
-    by_distance = sorted(range(1, side), key=lambda k: -min(k, side - k))
-
     def last_copy(c, part, k):
         spot = pl.ds(*ROUNDS[part])
         return remote(
@@ -429,7 +429,7 @@
             leaf_copy(k).wait()
             total = total + leaf_in[k]
         leaf_sum[...] = total
-        for k in range(1, side):
+        for k in by_distance:
             leaf_sum_copy(k).start()
 
     def leaf_second():
@@ -438,7 +438,7 @@
             leaf_sum_copy(k).wait()
             total = total + leaf_sum_in[k]
         value_own[...] = -total[:leaf_part] / (total[leaf_part:] + DAMPING)
-        for k in range(1, side):
+        for k in by_distance:
             value_copy(k).start()
 
     def leaf_third():

time: 57.6 us -> 57.5 us (level)
  no operation moved by 1% of the time
where the time goes in v5:
time: 57.5 us; the launch traced here: 57.3 us
  Pallas kernels  56.7 us (99%)
  between operations  0.64 us (1%)
    pallas_call x1, Pallas kernels, per_device(): pl.pallas_call(functools.partial(kernel, side, feat_total), out_shape=(ja...  54.5 us
    pallas_call x1, Pallas kernels, per_device(): pl.pallas_call(copy_kernel, out_shape=(jax.ShapeDtypeStruct(newp.shape, n...  2.21 us

profile of v5, /device:TPU:8, one launch (start us, length us, event | category | flops | bytes accessed | tf_op | source)
XLA Modules:
  0.0 57.3 jit_solution(1904905294271912442)
XLA Ops:
  0.6 54.5 %boost.1 = (bf16[1536,512]{1,0:T(8,128)(2,1)}, f32[4,2048]{1,0:T(4,128)}) custom-call(bf16[1536,512]{1,0:T(8,128)(2,1)} %pred_hbm.1, bf16[1536,512]{1,0:T(8,128)(2,1)} %targ_hbm.1, bf16[32,512]{1,0:T(8,128)(2,1)} %matrix_hbm.1, s32[32,1536]{1,0:T(8,128)} %codes_hbm.1, s32[1536]{0:T(1024)} %node_hbm.1, s32[4]{0:T(128)} %smaller_ref.1, s32[4]{0:T(128)} %feature_ref.1, ...), custom_call_target="tpu_custom_call" | custom-call | tf_op jit(solution)/shard_map/boost/pallas_call | solution.py:553
  55.1 2.2 %hand_on.1 = (bf16[1536,512]{1,0:T(8,128)(2,1)}, f32[4,2048]{1,0:T(4,128)}) custom-call(bf16[1536,512]{1,0:T(8,128)(2,1)} %get-tuple-element.4.newp_in, f32[4,2048]{1,0:T(4,128)} %get-tuple-element.5.hist_in), custom_call_target="tpu_custom_call" | custom-call | tf_op jit(solution)/shard_map/hand_on/pallas_call | solution.py:621
